TPU v7x, 32 devices: a whole 2x2x4 slice. The times are simulated.
32 devices in a mesh: grp: 2 (over x), pts: 16 (over z, y, core).
Axes of the slice: x: 2, y: 2, z: 4, core: 2. Of those that a mesh axis runs over, the one named last changes fastest.
Arguments:
- spectrum: float32 [1296, 8192], P(None, ('grp', 'pts')), parts along dimension 1, may hold values from 0.01 to 29, as said below
- wind_speed: float32 [8192], P(('grp', 'pts')), parts along dimension 0, may hold values from 0.5 to 3
- wind_dir: float32 [8192], P(('grp', 'pts')), parts along dimension 0, may hold values from -3.140625 to 3.140625
- turning: float32 [8192], P(('grp', 'pts')), parts along dimension 0, may hold values from -0.8 to 0.8
- sea_mask: int32 [48, 128], P('pts'), may hold values from 0 to 1, as said below
- band_start: int32 [16], replicated, may hold values from 0 to 4095, as said below
Outputs:
- updated: float32 [1296, 8192], P(None, ('grp', 'pts')), parts along dimension 1
There are 2 independent parts, one for each index of `grp`. A program takes and returns all parts, laid end to end along the dimension named above; an argument that names none is the same for every part. Nothing has to cross between parts.
Inputs may be any that keep to these rules, and one draw needn't show every extreme that they name: `spectrum`: spectrum entries are positive. `sea_mask`: there are exactly 4096 sea cells. Band b holds band_start[b + 1] - band_start[b] of them (the last band the rest up to 4096); every band holds at most 384 sea cells, and one band holds exactly that many. band_start[0] is 0 and band_start[b] is the number of sea cells in the rows before band b; every band holds at least one sea cell.
All inputs are finite; a program needn't handle non-finite values.
Results may differ from a plain program's by a relative error of at most 0.000076.
Values sent between devices are 32-bit elements; how exact they have to be, the bound alone decides.
A program may use at most 64 MiB of HBM per device.

v0:
```python
import math

import jax
import jax.numpy as jnp
from jax import lax
from jax.sharding import PartitionSpec as P

DIRS = 36
FREQS = 36


def padded_2(block, sides, width):
    for axis, dim in sides:
        count = lax.axis_size(axis)
        forward = [(i, i + 1) for i in range(count - 1)]
        backward = [(target, source) for source, target in forward]
        low = lax.ppermute(
            lax.slice_in_dim(block, block.shape[dim] - width, None, axis=dim), axis, forward
        )
        high = lax.ppermute(lax.slice_in_dim(block, 0, width, axis=dim), axis, backward)
        block = jnp.concatenate([low, block, high], axis=dim)
    return block


def spectral_tables():
    freq_steps = jnp.arange(FREQS, dtype=jnp.float32) / (FREQS - 1)
    frequency = 0.5 + 1.5 * freq_steps
    heading = 2.0 * math.pi / DIRS * jnp.arange(DIRS, dtype=jnp.float32)
    group_speed = 0.3 + 0.5 * freq_steps
    return (frequency, heading, group_speed)


def turning_matrix():
    row_ids = jnp.arange(DIRS)[:, None]
    col_ids = jnp.arange(DIRS)[None, :]
    ahead = (col_ids == (row_ids + 1) % DIRS).astype(jnp.float32)
    behind = (col_ids == (row_ids - 1) % DIRS).astype(jnp.float32)
    return 0.5 * ahead - 0.5 * behind


def source_terms(density, wind_speed, wind_dir, turning):
    frequency, heading, group_speed = spectral_tables()
    energy = jnp.mean(density, axis=0)
    shaped = density.reshape(FREQS, DIRS, -1)
    alignment = jnp.cos(heading[:, None] - wind_dir[None, :])
    growth = 0.2 * jax.nn.relu(wind_speed * alignment / frequency[:, None, None] - 0.3)
    decay = 0.1 * frequency[:, None, None] * energy
    sourced = shaped * jnp.exp(growth - decay)
    rotated = jnp.einsum("ts,fsx->ftx", turning_matrix(), sourced, precision=lax.Precision.HIGHEST)
    refracted = sourced - turning / frequency[:, None, None] * rotated
    return refracted.reshape(FREQS * DIRS, -1)


def advect(padded, cross, meridional):
    center = padded[:, 1:-1]
    south = padded[:, :-2]
    north = padded[:, 2:]
    western = jnp.roll(center, 1, axis=2)
    eastern = jnp.roll(center, -1, axis=2)
    return (
        center
        - jax.nn.relu(cross) * (center - western)
        - jnp.minimum(cross, 0.0) * (eastern - center)
        - jax.nn.relu(meridional) * (center - south)
        - jnp.minimum(meridional, 0.0) * (north - center)
    )


def shards(spectrum, wind_speed, wind_dir, turning, sea_mask, band_start):
    device_total = lax.axis_size("pts")
    own_band = lax.axis_index("pts")
    components, points = spectrum.shape
    band_rows, lon_cells = sea_mask.shape
    band_cells = band_rows * lon_cells
    slot_total = 3 * points // (2 * device_total)
    sea_total = points * device_total
    boundaries = jnp.concatenate([band_start, jnp.full((1,), sea_total, jnp.int32)])
    first_local = (boundaries - own_band + device_total - 1) // device_total
    slot_ids = jnp.arange(slot_total, dtype=jnp.int32)
    send_index = jnp.clip(first_local[:-1, None] + slot_ids[None, :], 0, points - 1).reshape(-1)
    flat_mask = sea_mask.reshape(-1)
    running = jnp.cumsum(flat_mask)
    band_first = band_start[own_band]
    sea_index = band_first + running - 1
    source_dev = sea_index % device_total
    source_first = (band_first - source_dev + device_total - 1) // device_total
    gather_index = jnp.clip(
        source_dev * slot_total + sea_index // device_total - source_first,
        0,
        device_total * slot_total - 1,
    )
    sea_float = flat_mask.astype(jnp.float32)

    def to_band(arrived):
        return jnp.take(arrived.reshape(arrived.shape[0], -1), gather_index, axis=1) * sea_float

    outgoing = jnp.take(spectrum, send_index, axis=1).reshape(components, device_total, slot_total)
    forcing = jnp.stack([wind_speed, wind_dir, turning])
    forcing_out = jnp.take(forcing, send_index, axis=1).reshape(3, device_total, slot_total)
    arrived, forcing_in = (
        lax.all_to_all(outgoing, "pts", split_axis=1, concat_axis=1, tiled=True),
        lax.all_to_all(forcing_out, "pts", split_axis=1, concat_axis=1, tiled=True),
    )
    band_forcing = to_band(forcing_in)
    updated = source_terms(to_band(arrived), band_forcing[0], band_forcing[1], band_forcing[2])
    layered = updated.reshape(components, band_rows, lon_cells)
    padded = padded_2(layered, (("pts", 1),), 1)
    frequency, heading, group_speed = spectral_tables()
    along = ((0.4 * group_speed)[:, None] * jnp.cos(heading)[None, :]).reshape(-1)
    across = ((0.35 * group_speed)[:, None] * jnp.sin(heading)[None, :]).reshape(-1)
    global_rows = (own_band * band_rows + jnp.arange(band_rows, dtype=jnp.int32)).astype(
        jnp.float32
    )
    latitude = (-60.0 + 120.0 * (global_rows + 0.5) / (band_rows * device_total)) * (
        math.pi / 180.0
    )
    cross = (along[:, None] / jnp.cos(latitude)[None, :])[:, :, None]
    advanced = advect(padded, cross, across[:, None, None]).reshape(components, band_cells)
    dest_ids = jnp.arange(device_total, dtype=jnp.int32)
    dest_first = (band_first - dest_ids + device_total - 1) // device_total
    back_sea = (dest_first[:, None] + slot_ids[None, :]) * device_total + dest_ids[:, None]
    positions = jnp.searchsorted(running, jnp.arange(band_cells, dtype=jnp.int32) + 1)
    positions = jnp.clip(positions, 0, band_cells - 1)
    back_index = positions[jnp.clip(back_sea - band_first, 0, band_cells - 1)].reshape(-1)
    returned = jnp.take(advanced, back_index, axis=1).reshape(components, device_total, slot_total)
    homecoming = lax.all_to_all(returned, "pts", split_axis=1, concat_axis=1, tiled=True)
    local_sea = jnp.arange(points, dtype=jnp.int32) * device_total + own_band
    band_of = jnp.sum((band_start[None, :] <= local_sea[:, None]).astype(jnp.int32), axis=1) - 1
    pick_index = jnp.clip(
        band_of * slot_total + jnp.arange(points, dtype=jnp.int32) - first_local[band_of],
        0,
        device_total * slot_total - 1,
    )
    return jnp.take(homecoming.reshape(components, -1), pick_index, axis=1)


def solution(mesh):
    placed = (
        P(None, ("grp", "pts")),
        P(("grp", "pts")),
        P(("grp", "pts")),
        P(("grp", "pts")),
        P("pts", None),
        P(),
    )
    return jax.shard_map(
        shards, mesh=mesh, in_specs=placed, out_specs=P(None, ("grp", "pts")), check_vma=False
    )
```

profile of v0, /device:TPU:15, one launch (start us, length us, event | category | flops | bytes accessed | tf_op | source)
XLA Modules:
  0.0 217.2 jit_solution(8978301247968551971)
XLA Ops:
  3.8 6.6 %all-to-all-start.1 = ((f32[3,16,24]{2,0,1:T(4,128)}), f32[3,16,24]{2,0,1:T(4,128)S(1)}, u32[]{:S(2)}, u32[]{:S(2)}) async-start(f32[3,16,24]{2,0,1:T(4,128)} %broadcast_select_fusion.2), calls=%async_computation.1 | async-start | bytes 65536 | tf_op jit(solution)/shard_map/all_to_all | solution.py:102
  14.7 2.7 %gather_fusion.1 = f32[384,1296]{1,0:T(8,128)} fusion(f32[1296,256]{0,1:T(8,128)S(1)} %copy.32, s32[1024]{0:T(1024)S(1)} %pad_clamp_fusion.5), kind=kCustom, calls=%fused_computation.3 | custom fusion | bytes 3982848 | tf_op jit(solution)/shard_map/jit(_take)/gather | solution.py:97
  17.4 3.2 %broadcast_select_fusion.1 = f32[1296,16,24]{0,2,1:T(8,128)} fusion(f32[1296,16,24]{0,2,1:T(8,128)} %bitcast.80, pred[16,24]{1,0:T(8,128)(4,1)S(1)} %compare_and_fusion), kind=kLoop, calls=%fused_computation.44 | loop fusion | flops 497664 | bytes 3981696 | tf_op jit(solution)/shard_map/jit(_take)/select_n | solution.py:97
  21.3 26.0 %while.24 = (s32[]{:T(128)}, u32[384]{0:T(512)S(1)}, u32[384]{0:T(512)S(1)}, s32[384]{0:T(512)S(1)}, s32[]{:T(128)}, /*index=5*/s32[]{:T(128)}, s32[]{}) while((s32[]{:T(128)}, u32[384]{0:T(512)S(1)}, u32[384]{0:T(512)S(1)}, s32[384]{0:T(512)S(1)}, s32[]{:T(128)}, /*index=5*/s32[]{:T(128)}, s32[]{}) %tuple.76), condition=%wide.region_5.7_spmd.clone, body=%wide.region_4.6_spmd.clone.sunk | while | flops 8324 | bytes 29541 | solution.py:122
  21.3 2.8 %gather_fusion = s32[384]{0:T(512)S(1)} fusion(s32[384]{0:T(512)S(1)} %get-tuple-element.204, u32[1024]{0:T(1024)S(1)} %pad_clamp_fusion.8), kind=kCustom, calls=%fused_computation.1.clone.clone.1 | custom fusion | bytes 4608 | tf_op jit(solution)/shard_map/jit(searchsorted)/jit(_searchsorted_scan_impl)/vmap(jit(_searchsorted_scan_impl))/while/body/eval_jaxpr/gather | solution.py:122
  24.2 2.8 %gather_fusion = s32[384]{0:T(512)S(1)} fusion(s32[384]{0:T(512)S(1)} %get-tuple-element.204, u32[1024]{0:T(1024)S(1)} %pad_clamp_fusion.8), kind=kCustom, calls=%fused_computation.1.clone.clone.1 | custom fusion | bytes 4608 | tf_op jit(solution)/shard_map/jit(searchsorted)/jit(_searchsorted_scan_impl)/vmap(jit(_searchsorted_scan_impl))/while/body/eval_jaxpr/gather | solution.py:122
  27.1 2.8 %gather_fusion = s32[384]{0:T(512)S(1)} fusion(s32[384]{0:T(512)S(1)} %get-tuple-element.204, u32[1024]{0:T(1024)S(1)} %pad_clamp_fusion.8), kind=kCustom, calls=%fused_computation.1.clone.clone.1 | custom fusion | bytes 4608 | tf_op jit(solution)/shard_map/jit(searchsorted)/jit(_searchsorted_scan_impl)/vmap(jit(_searchsorted_scan_impl))/while/body/eval_jaxpr/gather | solution.py:122
  30.0 2.8 %gather_fusion = s32[384]{0:T(512)S(1)} fusion(s32[384]{0:T(512)S(1)} %get-tuple-element.204, u32[1024]{0:T(1024)S(1)} %pad_clamp_fusion.8), kind=kCustom, calls=%fused_computation.1.clone.clone.1 | custom fusion | bytes 4608 | tf_op jit(solution)/shard_map/jit(searchsorted)/jit(_searchsorted_scan_impl)/vmap(jit(_searchsorted_scan_impl))/while/body/eval_jaxpr/gather | solution.py:122
  32.9 2.8 %gather_fusion = s32[384]{0:T(512)S(1)} fusion(s32[384]{0:T(512)S(1)} %get-tuple-element.204, u32[1024]{0:T(1024)S(1)} %pad_clamp_fusion.8), kind=kCustom, calls=%fused_computation.1.clone.clone.1 | custom fusion | bytes 4608 | tf_op jit(solution)/shard_map/jit(searchsorted)/jit(_searchsorted_scan_impl)/vmap(jit(_searchsorted_scan_impl))/while/body/eval_jaxpr/gather | solution.py:122
  35.8 2.8 %gather_fusion = s32[384]{0:T(512)S(1)} fusion(s32[384]{0:T(512)S(1)} %get-tuple-element.204, u32[1024]{0:T(1024)S(1)} %pad_clamp_fusion.8), kind=kCustom, calls=%fused_computation.1.clone.clone.1 | custom fusion | bytes 4608 | tf_op jit(solution)/shard_map/jit(searchsorted)/jit(_searchsorted_scan_impl)/vmap(jit(_searchsorted_scan_impl))/while/body/eval_jaxpr/gather | solution.py:122
  38.7 2.8 %gather_fusion = s32[384]{0:T(512)S(1)} fusion(s32[384]{0:T(512)S(1)} %get-tuple-element.204, u32[1024]{0:T(1024)S(1)} %pad_clamp_fusion.8), kind=kCustom, calls=%fused_computation.1.clone.clone.1 | custom fusion | bytes 4608 | tf_op jit(solution)/shard_map/jit(searchsorted)/jit(_searchsorted_scan_impl)/vmap(jit(_searchsorted_scan_impl))/while/body/eval_jaxpr/gather | solution.py:122
  41.6 2.8 %gather_fusion = s32[384]{0:T(512)S(1)} fusion(s32[384]{0:T(512)S(1)} %get-tuple-element.204, u32[1024]{0:T(1024)S(1)} %pad_clamp_fusion.8), kind=kCustom, calls=%fused_computation.1.clone.clone.1 | custom fusion | bytes 4608 | tf_op jit(solution)/shard_map/jit(searchsorted)/jit(_searchsorted_scan_impl)/vmap(jit(_searchsorted_scan_impl))/while/body/eval_jaxpr/gather | solution.py:122
  44.5 2.8 %gather_fusion = s32[384]{0:T(512)S(1)} fusion(s32[384]{0:T(512)S(1)} %get-tuple-element.204, u32[1024]{0:T(1024)S(1)} %pad_clamp_fusion.8), kind=kCustom, calls=%fused_computation.1.clone.clone.1 | custom fusion | bytes 4608 | tf_op jit(solution)/shard_map/jit(searchsorted)/jit(_searchsorted_scan_impl)/vmap(jit(_searchsorted_scan_impl))/while/body/eval_jaxpr/gather | solution.py:122
  47.6 6.0 %all-to-all-start = ((f32[1296,16,24]{0,2,1:T(8,128)}), f32[1296,16,24]{0,2,1:T(8,128)S(1)}, u32[]{:S(2)}, u32[]{:S(2)}) async-start(f32[1296,16,24]{0,2,1:T(8,128)} %broadcast_select_fusion.1), calls=%async_computation | async-start | bytes 4325376 | tf_op jit(solution)/shard_map/all_to_all | solution.py:101
  56.8 2.8 %gather_fusion.4 = s32[384]{0:T(512)S(1)} fusion(s32[384]{0:T(512)S(1)} %convert_clamp_fusion, s32[1024]{0:T(1024)S(1)} %pad_clamp_fusion.6), kind=kCustom, calls=%fused_computation.6 | custom fusion | bytes 4608 | tf_op jit(solution)/shard_map/gather | solution.py:124
  63.2 39.2 %all-to-all-done = f32[1296,16,24]{0,2,1:T(8,128)S(1)} async-done(((f32[1296,16,24]{0,2,1:T(8,128)}), f32[1296,16,24]{0,2,1:T(8,128)S(1)}, u32[]{:S(2)}, u32[]{:S(2)}) %all-to-all-start) | async-done | bytes 1990688 | tf_op jit(solution)/shard_map/all_to_all | solution.py:101
  102.4 2.7 %gather_fusion.6 = f32[384,1296]{1,0:T(8,128)} fusion(f32[1296,384]{0,1:T(8,128)S(1)} %bitcast.77, s32[1024]{0:T(1024)S(1)} %pad_clamp_fusion.4), kind=kCustom, calls=%fused_computation.clone | custom fusion | bytes 3982848 | tf_op jit(solution)/shard_map/jit(_take)/gather | solution.py:95
  105.1 2.0 fusion.49
  110.7 4.7 %bitcast_subtract_fusion = f32[36,36,384]{2,1,0:T(8,128)} fusion(f32[36,36,384]{2,1,0:T(8,128)S(1)} %reshape.702, f32[36,384]{1,0:T(8,128)S(1)} %get-tuple-element.151, f32[36,384]{1,0:T(8,128)S(1)} %broadcast_multiply_fusion, f32[36]{0:T(128)S(1)} %multiply_add_fusion.2, f32[36,384]{1,0:T(8,128)S(1)} %get-tuple-element.150, s32[36]{0:T(128)S(1)} %get-tuple-element.152, ...), kind=kOutput, calls=%fused_computation.34 | convolution fusion | flops 221964624 | bytes 4147632 | tf_op jit(solution)/shard_map/ts,fsx->ftx/dot_general | solution.py:49
  115.4 2.8 %reshape_reshape.3 = f32[1296,3,128]{2,1,0:T(4,128)S(1)} reshape(f32[36,36,384]{2,1,0:T(8,128)} %bitcast_subtract_fusion) | data formatting | bytes 3981312 | tf_op jit(solution)/shard_map/reshape;reshape | solution.py:106
  119.3 3.6 %collective-permute-start = (f32[1296,1,128]{2,1,0:T(1,128)S(1)}, f32[1296,1,128]{2,1,0:T(1,128)S(1)}, u32[]{:S(2)}, u32[]{:S(2)}) collective-permute-start(f32[1296,1,128]{2,1,0:T(1,128)S(1)} %get-tuple-element.125), channel_id=1, source_target_pairs={{0,1},{1,2},{2,3},{3,4},{4,5},{5,6},{6,7},{7,8},{8,9},{9,10},{10,1... | collective-permute-start | bytes 1990664 | tf_op jit(solution)/shard_map/ppermute | solution.py:17
  122.9 2.1 collective-permute-start.1
  130.6 5.4 %collective-permute-done.1 = f32[1296,1,128]{2,1,0:T(1,128)S(1)} collective-permute-done((f32[1296,1,128]{2,1,0:T(1,128)S(1)}, f32[1296,1,128]{2,1,0:T(1,128)S(1)}, u32[]{:S(2)}, u32[]{:S(2)}) %collective-permute-start.1) | collective-permute-done | bytes 663584 | tf_op jit(solution)/shard_map/ppermute | solution.py:20
  135.9 10.8 %fusion.4 = f32[1296,3,128]{2,1,0:T(4,128)} fusion(f32[1296,3,128]{2,1,0:T(4,128)S(1)} %reshape_reshape.3, f32[1296,1,128]{2,1,0:T(1,128)S(1)} %collective-permute-done.1, f32[1296,1,128]{2,1,0:T(1,128)S(1)} %collective-permute-done, f32[1296,3,127]{2,1,0:T(4,128)S(1)} %get-tuple-element.122, f32[1296,3,1]{2,1,0:T(4,128)S(1)} %get-tuple-element.124, ...), kind=kLoop, calls=%fused_computation.17 | loop fusion | flops 7962624 | bytes 9331200 | tf_op jit(solution)/shard_map/sub | solution.py:61
  146.7 3.0 %copy.39 = f32[1296,3,128]{0,2,1:T(8,128)S(1)} copy(f32[1296,3,128]{2,1,0:T(4,128)} %fusion.4) | data formatting | bytes 3981312 | tf_op jit(solution)/shard_map/sub | solution.py:61
  149.7 2.7 %gather_fusion.7 = f32[384,1296]{1,0:T(8,128)} fusion(f32[1296,384]{0,1:T(8,128)S(1)} %bitcast.76, s32[1024]{0:T(1024)S(1)} %pad_clamp_fusion.2), kind=kCustom, calls=%fused_computation.2.clone | custom fusion | bytes 3982848 | tf_op jit(solution)/shard_map/jit(_take)/gather | solution.py:125
  152.4 3.2 %broadcast_select_fusion = f32[384,1296]{1,0:T(8,128)} fusion(f32[384,1296]{1,0:T(8,128)} %gather_fusion.7, pred[384]{0:T(512)(128)(4,1)S(1)} %compare_and_fusion.1), kind=kLoop, calls=%fused_computation.43 | loop fusion | flops 497664 | bytes 3981696 | tf_op jit(solution)/shard_map/jit(_take)/select_n | solution.py:125
  155.6 7.4 %all-to-all-start.2 = ((f32[1296,16,24]{0,2,1:T(8,128)}), f32[1296,16,24]{0,2,1:T(8,128)S(1)}, u32[]{:S(2)}, u32[]{:S(2)}) async-start(f32[1296,16,24]{0,2,1:T(8,128)} %bitcast.79), calls=%async_computation.2 | async-start | bytes 4325376 | tf_op jit(solution)/shard_map/all_to_all | solution.py:126
  163.9 4.3 %compare_select_fusion.8 = (s32[256,1]{0,1:T(1,128)S(1)}, s32[256,1]{0,1:T(1,128)S(1)}) fusion(s32[]{:T(128)} %bitcast.12, s32[]{:T(128)} %bitcast.13, s32[]{:T(128)} %bitcast.14, s32[]{:T(128)} %bitcast.15, s32[]{:T(128)} %bitcast.16, s32[]{:T(128)} %bitcast.18, s32[]{:T(128)} %bitcast.17, s32[256,1]{0,1:T(1,128)S(1)} %bitcast.89, s32[256,1]{0,1:T(1,128)S(1)} %bitcast.85), kind=kLoop, calls=%fused_computation.100 | loop fusion | flops 3584 | bytes 4124 | tf_op jit(solution)/shard_map/gather | solution.py:130
  168.2 6.3 %compare_and_fusion.3 = (pred[256]{0:T(512)(128)(4,1)S(1)}, s32[256]{0:T(256)S(1)}) fusion(s32[256]{0:T(256)S(1)} %convert_reduce_fusion, pred[256]{0:T(512)(128)(4,1)S(1)} %get-tuple-element.101, pred[256]{0:T(512)(128)(4,1)S(1)} %get-tuple-element.100, pred[256]{0:T(512)(128)(4,1)S(1)} %get-tuple-element.99, pred[256]{0:T(512)(128)(4,1)S(1)} %get-tuple-element.98, ...), kind=kLoop, calls=%fused_computation.141 | loop fusion | flops 5376 | bytes 5928 | tf_op jit(solution)/shard_map/jit(_take)/and | solution.py:134
  174.6 37.3 %all-to-all-done.2 = f32[1296,16,24]{0,2,1:T(8,128)S(1)} async-done(((f32[1296,16,24]{0,2,1:T(8,128)}), f32[1296,16,24]{0,2,1:T(8,128)S(1)}, u32[]{:S(2)}, u32[]{:S(2)}) %all-to-all-start.2) | async-done | bytes 1990688 | tf_op jit(solution)/shard_map/all_to_all | solution.py:126
  211.9 2.3 %gather_fusion.5 = f32[256,1296]{1,0:T(8,128)} fusion(f32[1296,384]{0,1:T(8,128)S(1)} %bitcast.78, s32[1024]{0:T(1024)S(1)} %pad_clamp_fusion.1), kind=kCustom, calls=%fused_computation.7 | custom fusion | bytes 2655232 | tf_op jit(solution)/shard_map/jit(_take)/gather | solution.py:134
  (122 shorter events, 30.1 us)
Async XLA Ops:
  3.8 43.7 %all-to-all-start.1 = ((f32[3,16,24]{2,0,1:T(4,128)}), f32[3,16,24]{2,0,1:T(4,128)S(1)}, u32[]{:S(2)}, u32[]{:S(2)}) async-start(f32[3,16,24]{2,0,1:T(4,128)} %broadcast_select_fusion.2), calls=%async_computation.1 | async-start | bytes 65536 | tf_op jit(solution)/shard_map/all_to_all | solution.py:102
  47.6 54.9 %all-to-all-start = ((f32[1296,16,24]{0,2,1:T(8,128)}), f32[1296,16,24]{0,2,1:T(8,128)S(1)}, u32[]{:S(2)}, u32[]{:S(2)}) async-start(f32[1296,16,24]{0,2,1:T(8,128)} %broadcast_select_fusion.1), calls=%async_computation | async-start | bytes 4325376 | tf_op jit(solution)/shard_map/all_to_all | solution.py:101
  56.8 4.3 %copy-start.1 = (s32[3,128]{1,0:T(4,128)S(1)}, s32[3,128]{1,0:T(4,128)}, u32[]{:S(2)}) copy-start(s32[3,128]{1,0:T(4,128)} %param.14) | copy-start | bytes 4612
  119.3 11.2 %collective-permute-start = (f32[1296,1,128]{2,1,0:T(1,128)S(1)}, f32[1296,1,128]{2,1,0:T(1,128)S(1)}, u32[]{:S(2)}, u32[]{:S(2)}) collective-permute-start(f32[1296,1,128]{2,1,0:T(1,128)S(1)} %get-tuple-element.125), channel_id=1, source_target_pairs={{0,1},{1,2},{2,3},{3,4},{4,5},{5,6},{6,7},{7,8},{8,9},{9,10},{10,1... | collective-permute-start | bytes 1990664 | tf_op jit(solution)/shard_map/ppermute | solution.py:17
  122.9 13.0 %collective-permute-start.1 = (f32[1296,1,128]{2,1,0:T(1,128)S(1)}, f32[1296,1,128]{2,1,0:T(1,128)S(1)}, u32[]{:S(2)}, u32[]{:S(2)}) collective-permute-start(f32[1296,1,128]{2,1,0:T(1,128)S(1)} %get-tuple-element.126), channel_id=1, source_target_pairs={{1,0},{2,1},{3,2},{4,3},{5,4},{6,5},{7,6},{8,7},{9,8},{10,9},{11,1... | collective-permute-start | bytes 1990664 | tf_op jit(solution)/shard_map/ppermute | solution.py:20
  126.9 9.1 %copy-start = (f32[1296,3]{1,0:T(8,128)S(1)}, f32[1296,3]{1,0:T(8,128)}, u32[]{:S(2)}) copy-start(f32[1296,3]{1,0:T(8,128)} %copy.38) | copy-start | bytes 46660
  155.6 8.1 %copy-start.2 = (s32[16]{0:T(128)S(1)}, s32[16]{0:T(128)}, u32[]{:S(2)}) copy-start(s32[16]{0:T(128)} %param.15) | copy-start | bytes 196
  155.6 56.3 %all-to-all-start.2 = ((f32[1296,16,24]{0,2,1:T(8,128)}), f32[1296,16,24]{0,2,1:T(8,128)S(1)}, u32[]{:S(2)}, u32[]{:S(2)}) async-start(f32[1296,16,24]{0,2,1:T(8,128)} %bitcast.79), calls=%async_computation.2 | async-start | bytes 4325376 | tf_op jit(solution)/shard_map/all_to_all | solution.py:126
where the time goes:
time: 218 us; the launch traced here: 217 us
  waiting for transfers between devices  83.7 us (38%)
  local copies, waits for them, and re-layouts  62.8 us (29%)
  other arithmetic  39.4 us (18%)
  starting transfers between devices  25.7 us (12%)
  matrix products  4.73 us (2%)
    all_to_all x1, waiting for transfers between devices, shards(): lax.all_to_all(outgoing, 'pts', split_axis=1, concat_axis=1, tiled=True)  39.2 us
    all_to_all x1, waiting for transfers between devices, shards(): lax.all_to_all(returned, 'pts', split_axis=1, concat_axis=1, tiled=True)  37.3 us
    gather x9, local copies, waits for them, and re-layouts, shards(): jnp.searchsorted(running, jnp.arange(band_cells, dtype=jnp.int32) + 1)  25.2 us
    sub x1, other arithmetic, advect(): center - jax.nn.relu(cross) * (center - western)  10.8 us
    all_to_all x1, starting transfers between devices, shards(): lax.all_to_all(returned, 'pts', split_axis=1, concat_axis=1, tiled=True)  7.43 us
    all_to_all x1, starting transfers between devices, shards(): lax.all_to_all(forcing_out, 'pts', split_axis=1, concat_axis=1, tiled=True)  6.55 us
    and x1, other arithmetic, shards(): return jnp.take(homecoming.reshape(components, -1), pick_index, axis=1)  6.3 us
    all_to_all x1, starting transfers between devices, shards(): lax.all_to_all(outgoing, 'pts', split_axis=1, concat_axis=1, tiled=True)  6.03 us
  transfers between devices with their start and end apart: 5, of which 4 were waited for; matrix products, arithmetic and copies ran while one was open for 28% of the time, Pallas kernels for 0%

commit v1 on v0

v1 whole, which is shorter than its diff:
```python
import functools
import math

import jax
import jax.numpy as jnp
import numpy as np
from jax import lax
from jax.experimental import pallas as pl
from jax.experimental.pallas import tpu as pltpu
from jax.sharding import PartitionSpec as P

DIRS = 36
FREQS = 36
PAIR = 2 * DIRS
LANES = 128
CHUNK = 16
MESH = pl.DeviceIdType.MESH


def spectral_tables():
    heading = 2.0 * np.pi / DIRS * np.arange(DIRS)
    group_speed = 0.3 + 0.5 * np.arange(FREQS) / (FREQS - 1)
    along = ((0.4 * group_speed)[:, None] * np.cos(heading)[None, :]).reshape(-1, 1)
    across = ((0.35 * group_speed)[:, None] * np.sin(heading)[None, :]).reshape(-1, 1)
    wide = lambda v, lanes: np.ascontiguousarray(np.broadcast_to(v, (v.shape[0], lanes))).astype(np.float32)
    cos2 = np.tile(np.cos(heading), 2)[:, None]
    sin2 = np.tile(np.sin(heading), 2)[:, None]
    ids = np.arange(DIRS)
    turn = 0.5 * (ids[None, :] == (ids[:, None] + 1) % DIRS) - 0.5 * (ids[None, :] == (ids[:, None] - 1) % DIRS)
    turn2 = np.kron(np.eye(2), turn).astype(np.float32)
    return wide(along, LANES), wide(across, LANES), wide(cos2, LANES), wide(sin2, LANES), turn2


def lane_take(x, idx):
    return jnp.take_along_axis(x, idx, axis=1, mode="promise_in_bounds")


def granule_transpose(tiles, granule, lane):
    tiles = list(tiles)
    step = 1
    while step < len(tiles):
        keep = (lane // granule) & step == 0
        for d in range(len(tiles)):
            if d & step == 0:
                a, b = tiles[d], tiles[d | step]
                width = step * granule
                tiles[d] = jnp.where(keep, a, pltpu.roll(b, width, 1))
                tiles[d | step] = jnp.where(keep, pltpu.roll(a, LANES - width, 1), b)
        step *= 2
    return tiles


def kernel(n, spec, speed, wdir, turning, mask, along, across, cos2, sin2, turn2, lat,
           out, refr, arrived, result, ex_in, ex_out, aligned, slots, cells, rolled, tabs, lat_tab, grid,
           mask_send, mask_recv, fwd_send, fwd_recv, back_send, back_recv,
           exf_send, exf_recv, exb_send, exb_recv):
    me = lax.axis_index("pts")
    comps, points = spec.shape
    band_rows = mask.shape[0]
    rows = band_rows * n
    tiles = points * n // LANES
    halves = points // LANES
    granule = LANES // n
    log_n = n.bit_length() - 1
    groups = comps // 8
    per_dev = groups // n * 8
    chunks = per_dev // CHUNK
    extra = groups - n * (per_dev // 8)
    base = 8 * extra

    def peer(i):
        return lax.rem(me + i, n)

    def each_peer(body):
        def step(i, carry):
            body(peer(i))
            return carry
        lax.fori_loop(1, n, step, 0)

    def remote(src, dst, send, recv, dev):
        return pltpu.make_async_remote_copy(src_ref=src, dst_ref=dst, send_sem=send, recv_sem=recv,
                                            device_id={"pts": dev}, device_id_type=MESH)

    def wait_bytes(ref, sem):
        pltpu.make_async_copy(ref, ref, sem).wait()

    def rows_of(start, count):
        return pl.ds(pl.multiple_of(start, 8), count)

    barrier = pltpu.get_barrier_semaphore()
    each_peer(lambda p: pl.semaphore_signal(barrier, inc=1, device_id={"pts": p}, device_id_type=MESH))
    slots[me] = jnp.zeros((8, LANES), jnp.float32)
    slots[me, 0:band_rows, :] = mask[...].astype(jnp.float32)

    cos_w = speed[...] * jnp.cos(wdir[...])
    sin_w = speed[...] * jnp.sin(wdir[...])
    aligned[...] = cos2[:, 0:1] * cos_w + sin2[:, 0:1] * sin_w
    energy = jnp.sum(spec[...].reshape(comps // 8, 8, points), axis=0)
    energy = jnp.sum(energy, axis=0, keepdims=True) * (0.1 / comps)
    turn_col = turning[...]
    second = lax.broadcasted_iota(jnp.int32, (PAIR, points), 0) >= DIRS

    pl.semaphore_wait(barrier, n - 1)
    each_peer(lambda p: remote(slots.at[me], slots.at[me], mask_send, mask_recv, p).start())

    def source(i, carry):
        at = rows_of(i * PAIR, PAIR)
        freq = 0.5 + (3.0 / (FREQS - 1)) * i.astype(jnp.float32)
        sigma = jnp.where(second, freq + 1.5 / (FREQS - 1), freq)
        inv = 1.0 / sigma
        growth = 0.2 * jnp.maximum(aligned[...] * inv - 0.3, 0.0)
        x = spec[at, :] * jnp.exp(growth - sigma * energy)
        rot = jnp.dot(turn2[...], x, precision=lax.Precision.HIGHEST, preferred_element_type=jnp.float32)
        refr[at, :] = x - turn_col * inv * rot
        return carry

    done = 0

    def source_to(row_end, done):
        need = -(-row_end // PAIR)
        if need > done:
            lax.fori_loop(done, need, source, 0)
        return max(need, done)

    done = source_to(base, done)
    for p in range(extra):
        @pl.when(me != p)
        def _():
            remote(refr.at[pl.ds(8 * p, 8)], ex_in.at[me], exf_send.at[p], exf_recv, p).start()

        @pl.when(me == p)
        def _():
            ex_in[me] = refr[8 * p:8 * p + 8, :]
    for c in range(chunks):
        first = base + c * CHUNK * n
        done = source_to(first + CHUNK * n, done)
        each_peer(lambda p: remote(refr.at[rows_of(first + CHUNK * p, CHUNK)], arrived.at[c, me],
                                   fwd_send.at[c], fwd_recv.at[c], p).start())
        arrived[c, me] = refr[rows_of(first + CHUNK * me, CHUNK), :]

    others = pl.ds(0, n - 1)
    wait_bytes(slots.at[others], mask_recv)
    for b in range(n):
        cells[band_rows * b:band_rows * (b + 1), :] = slots[b, 0:band_rows, :]
    m = cells[...]
    tri = (lax.broadcasted_iota(jnp.int32, (LANES, LANES), 0)
           < lax.broadcasted_iota(jnp.int32, (LANES, LANES), 1)).astype(jnp.float32)
    low = (lax.broadcasted_iota(jnp.int32, (rows, rows), 1)
           < lax.broadcasted_iota(jnp.int32, (rows, rows), 0)).astype(jnp.float32)
    rank = jnp.dot(m, tri, preferred_element_type=jnp.float32).astype(jnp.int32)
    before = jnp.dot(low, m, preferred_element_type=jnp.float32)
    begin = jnp.broadcast_to(jnp.sum(before, axis=1, keepdims=True), m.shape).astype(jnp.int32)
    count = jnp.broadcast_to(jnp.sum(m, axis=1, keepdims=True), m.shape).astype(jnp.int32)
    sea = m > 0.5
    lane = lax.broadcasted_iota(jnp.int32, (rows, LANES), 1)
    row = lax.broadcasted_iota(jnp.int32, (rows, LANES), 0)
    index = jnp.where(sea, begin + rank, -1)
    west = pltpu.roll(index, 1, 1)
    east = pltpu.roll(index, LANES - 1, 1)
    south = jnp.where(row == 0, -1, pltpu.roll(index, 1, 0))
    north = jnp.where(row == rows - 1, -1, pltpu.roll(index, rows - 1, 0))
    col = jnp.where(sea, lane, -1)
    shift = jnp.where(sea, lane - rank, 0)
    for bit in range(7):
        width = 1 << bit
        col_m = pltpu.roll(col, LANES - width, 1)
        shift_m = pltpu.roll(shift, LANES - width, 1)
        take = (col_m >= 0) & (((shift_m >> bit) & 1) == 1)
        stay = (col >= 0) & (((shift >> bit) & 1) == 0)
        col = jnp.where(take, col_m, jnp.where(stay, col, -1))
        shift = jnp.where(take, shift_m, shift)
    source_col = jnp.maximum(lane_take(col, (lane - begin) & (LANES - 1)), 0)
    for i, table in enumerate((west, east, south, north)):
        rolled[i] = lane_take(table, source_col)
    rolled[4] = begin
    rolled[5] = begin + count

    q_tile = lax.broadcasted_iota(jnp.int32, (tiles, LANES), 0)
    q_lane = lax.broadcasted_iota(jnp.int32, (tiles, LANES), 1)
    q = q_tile * LANES + q_lane

    def spread(r, carry):
        at = pl.ds(r, 1)
        inside = (q >= rolled[4, at, :]) & (q < rolled[5, at, :])
        pieces = [jnp.where(inside, rolled[i, at, :], carry[i]) for i in range(4)]
        return (*pieces, jnp.where(inside, lat[at, :], carry[4]))

    zero = jnp.zeros((tiles, LANES), jnp.int32)
    found = lax.fori_loop(0, rows, spread, (zero, zero, zero, zero, zero.astype(jnp.float32)))
    order = (q_lane & (granule - 1)) * n + q_lane // granule
    for i in range(4):
        near = found[i]
        code = (((near >> 7) - q_tile + 1) * LANES + granule * (near & (n - 1))
                + ((near & (LANES - 1)) >> log_n))
        code = lane_take(jnp.where(near < 0, 3 * LANES, code), order)
        for t in range(tiles):
            tabs[t, i] = jnp.broadcast_to(code[t:t + 1, :], (8, LANES))
    inverse_lat = lane_take(found[4], order)
    for t in range(tiles):
        lat_tab[t] = jnp.broadcast_to(inverse_lat[t:t + 1, :], (8, LANES))

    lane8 = lax.broadcasted_iota(jnp.int32, (8, LANES), 1)

    def advance(src, dst, sub, first_row):
        at = pl.ds(8 * sub, 8)
        for h in range(halves):
            part = pl.ds(h * LANES, LANES)
            moved = granule_transpose([src[d, at, part] for d in range(n)], granule, lane8)
            for t in range(n):
                grid[sub, h * n + t] = moved[t]
        zonal = along[rows_of(first_row, 8), :]
        merid = across[rows_of(first_row, 8), :]
        from_west = zonal > 0.0
        from_south = merid > 0.0
        zonal, merid = jnp.abs(zonal), jnp.abs(merid)

        def pick(code, prev, cur, nxt):
            where = code & (LANES - 1)
            tile = code >> 7
            got = jnp.where(tile == 1, lane_take(cur, where), 0.0)
            got = jnp.where(tile == 0, lane_take(prev, where), got)
            return jnp.where(tile == 2, lane_take(nxt, where), got)

        for h in range(halves):
            new = []
            for u in range(n):
                t = h * n + u
                prev, cur, nxt = grid[sub, max(t - 1, 0)], grid[sub, t], grid[sub, min(t + 1, tiles - 1)]
                beside = pick(jnp.where(from_west, tabs[t, 0], tabs[t, 1]), prev, cur, nxt)
                behind = pick(jnp.where(from_south, tabs[t, 2], tabs[t, 3]), prev, cur, nxt)
                new.append(cur - zonal * lat_tab[t] * (cur - beside) - merid * (cur - behind))
            moved = granule_transpose(new, granule, lane8)
            part = pl.ds(h * LANES, LANES)
            for d in range(n):
                dst[d, at, part] = moved[d]

    if extra:
        @pl.when(me < extra)
        def _():
            wait_bytes(ex_in.at[others], exf_recv)
            advance(ex_in, ex_out, 0, 8 * me)
            each_peer(lambda p: remote(ex_out.at[p], out.at[rows_of(8 * me, 8)], exb_send, exb_recv.at[me], p).start())
            out[rows_of(8 * me, 8), :] = ex_out[me]

    def one_chunk(c, carry):
        wait_bytes(arrived.at[c, others], fwd_recv.at[c])
        mine = base + c * CHUNK * n + CHUNK * me
        for sub in range(CHUNK // 8):
            advance(arrived.at[c], result.at[c], sub, mine + 8 * sub)
        each_peer(lambda p: remote(result.at[c, p], out.at[rows_of(mine, CHUNK)],
                                   back_send.at[c], back_recv.at[c], p).start())
        out[rows_of(mine, CHUNK), :] = result[c, me]
        return carry

    lax.fori_loop(0, chunks, one_chunk, 0)

    wait_bytes(slots.at[others], mask_send)
    for c in range(chunks):
        wait_bytes(arrived.at[c, others], fwd_send.at[c])
        wait_bytes(result.at[c, others], back_send.at[c])
        wait_bytes(result.at[c, others], back_recv.at[c])
    if extra:
        for p in range(extra):
            @pl.when(me != p)
            def _():
                wait_bytes(ex_in.at[0], exf_send.at[p])
                wait_bytes(ex_in.at[0], exb_recv.at[p])

        @pl.when(me < extra)
        def _():
            wait_bytes(ex_out.at[others], exb_send)


def shards(n, spectrum, wind_speed, wind_dir, turning, sea_mask, band_start):
    comps, points = spectrum.shape
    band_rows = sea_mask.shape[0]
    rows = band_rows * n
    tiles = points * n // LANES
    groups = comps // 8
    chunks = max(groups // n * 8 // CHUNK, 1)
    extra = max(groups - n * (groups // n), 1)
    latitude = (-60.0 + 120.0 * (np.arange(rows) + 0.5) / rows) * (math.pi / 180.0)
    lat = np.ascontiguousarray(np.broadcast_to((1.0 / np.cos(latitude))[:, None], (rows, LANES))).astype(np.float32)
    vmem = pl.BlockSpec(memory_space=pltpu.VMEM)
    dma = pltpu.SemaphoreType.DMA
    f32, i32 = jnp.float32, jnp.int32
    call = pl.pallas_call(
        functools.partial(kernel, n),
        out_shape=jax.ShapeDtypeStruct((comps, points), f32),
        in_specs=[vmem] * 11,
        out_specs=vmem,
        scratch_shapes=[
            pltpu.VMEM((comps, points), f32),
            pltpu.VMEM((chunks, n, CHUNK, points), f32),
            pltpu.VMEM((chunks, n, CHUNK, points), f32),
            pltpu.VMEM((n, 8, points), f32),
            pltpu.VMEM((n, 8, points), f32),
            pltpu.VMEM((PAIR, points), f32),
            pltpu.VMEM((n, 8, LANES), f32),
            pltpu.VMEM((rows, LANES), f32),
            pltpu.VMEM((6, rows, LANES), i32),
            pltpu.VMEM((tiles, 4, 8, LANES), i32),
            pltpu.VMEM((tiles, 8, LANES), f32),
            pltpu.VMEM((CHUNK // 8, tiles, 8, LANES), f32),
            dma, dma,
            dma((chunks,)), dma((chunks,)), dma((chunks,)), dma((chunks,)),
            dma((extra,)), dma, dma, dma((extra,)),
        ],
        compiler_params=pltpu.CompilerParams(
            collective_id=0, has_side_effects=True, vmem_limit_bytes=40 * 1024 * 1024
        ),
    )
    line = lambda v: v.reshape(1, points)
    return call(spectrum, line(wind_speed), line(wind_dir), line(turning), sea_mask, *spectral_tables(), lat)


def solution(mesh):
    placed = (
        P(None, ("grp", "pts")),
        P(("grp", "pts")),
        P(("grp", "pts")),
        P(("grp", "pts")),
        P("pts", None),
        P(),
    )
    return jax.shard_map(
        functools.partial(shards, mesh.shape["pts"]), mesh=mesh, in_specs=placed,
        out_specs=P(None, ("grp", "pts")), check_vma=False
    )
```

time: 218 us -> 75.4 us (0.35)
  the two profiles are of different devices: /device:TPU:15 before, /device:TPU:0 now
where the time goes in v1:
time: 75.4 us; the launch traced here: 74.2 us
  Pallas kernels  63.9 us (85%)
  local copies, waits for them, and re-layouts  10.3 us (14%)
    pallas_call x1, Pallas kernels, shards(): call(spectrum, line(wind_speed), line(wind_dir), line(turning), sea_mask,...  63.9 us
    unnamed x23, local copies, waits for them, and re-layouts  10.3 us

profile of v1, /device:TPU:0, one launch (start us, length us, event | category | flops | bytes accessed | tf_op | source)
XLA Modules:
  0.0 74.2 jit_solution(16184474991742296882)
XLA Ops:
  0.0 0.0 copy-start
  0.0 1.3 %copy-done = f32[1296,256]{1,0:T(8,128)S(1)} copy-done((f32[1296,256]{1,0:T(8,128)S(1)}, f32[1296,256]{1,0:T(8,128)}, u32[]{:S(2)}) %copy-start) | copy-done | bytes 1327128
  1.3 0.0 copy-start.1
  1.3 1.1 %copy-done.1 = f32[1296,128]{1,0:T(8,128)S(1)} copy-done((f32[1296,128]{1,0:T(8,128)S(1)}, f32[1296,128]{1,0:T(8,128)}, u32[]{:S(2)}) %copy-start.1) | copy-done | bytes 663576
  2.4 0.0 copy-start.2
  2.4 1.1 %copy-done.2 = f32[1296,128]{1,0:T(8,128)S(1)} copy-done((f32[1296,128]{1,0:T(8,128)S(1)}, f32[1296,128]{1,0:T(8,128)}, u32[]{:S(2)}) %copy-start.2) | copy-done | bytes 663576
  3.5 0.0 copy-start.3
  3.5 0.8 %copy-done.3 = f32[72,72]{1,0:T(8,128)S(1)} copy-done((f32[72,72]{1,0:T(8,128)S(1)}, f32[72,72]{1,0:T(8,128)}, u32[]{:S(2)}) %copy-start.3) | copy-done | bytes 20760
  4.3 0.0 copy-start.4
  4.3 0.8 %copy-done.4 = f32[72,128]{1,0:T(8,128)S(1)} copy-done((f32[72,128]{1,0:T(8,128)S(1)}, f32[72,128]{1,0:T(8,128)}, u32[]{:S(2)}) %copy-start.4) | copy-done | bytes 36888
  5.0 0.0 copy-start.5
  5.0 0.8 %copy-done.5 = f32[72,128]{1,0:T(8,128)S(1)} copy-done((f32[72,128]{1,0:T(8,128)S(1)}, f32[72,128]{1,0:T(8,128)}, u32[]{:S(2)}) %copy-start.5) | copy-done | bytes 36888
  5.8 0.0 copy-start.6
  5.8 0.7 copy-done.6
  6.5 0.0 copy-start.7
  6.5 0.7 copy-done.7
  7.2 0.0 copy-start.8
  7.2 0.7 copy-done.8
  7.9 0.0 copy-start.9
  7.9 0.7 copy-done.9
  8.6 0.0 copy-start.10
  8.6 0.7 copy-done.10
  9.3 63.9 %shard_map.109 = f32[1296,256]{1,0:T(8,128)S(1)} custom-call(f32[1296,256]{1,0:T(8,128)S(1)} %copy-done, f32[1,256]{1,0:T(1,128)S(1)} %bitcast.3, f32[1,256]{1,0:T(1,128)S(1)} %bitcast.4, f32[1,256]{1,0:T(1,128)S(1)} %bitcast.5, s32[3,128]{1,0:T(4,128)S(1)} %copy-done.7, f32[1296,128]{1,0:T(8,128)S(1)} %copy-done.2, f32[1296,128]{1,0:T(8,128)S(1)} %copy-done.1, ...), custom_call_target="tpu_custom_call" | custom-call | tf_op jit(solution)/shard_map/pallas_call | solution.py:314
  73.2 1.1 %copy.13 = f32[1296,256]{1,0:T(8,128)} copy(f32[1296,256]{1,0:T(8,128)S(1)} %shard_map.109) | data formatting | bytes 2654208
Async XLA Ops:
  0.0 1.3 %copy-start = (f32[1296,256]{1,0:T(8,128)S(1)}, f32[1296,256]{1,0:T(8,128)}, u32[]{:S(2)}) copy-start(f32[1296,256]{1,0:T(8,128)} %spec.1) | copy-start | bytes 3981316
  1.3 1.1 %copy-start.1 = (f32[1296,128]{1,0:T(8,128)S(1)}, f32[1296,128]{1,0:T(8,128)}, u32[]{:S(2)}) copy-start(f32[1296,128]{1,0:T(8,128)} %constant.13.clone.across) | copy-start | bytes 1990660
  2.4 1.1 %copy-start.2 = (f32[1296,128]{1,0:T(8,128)S(1)}, f32[1296,128]{1,0:T(8,128)}, u32[]{:S(2)}) copy-start(f32[1296,128]{1,0:T(8,128)} %constant.12.clone.along) | copy-start | bytes 1990660
  3.5 0.8 %copy-start.3 = (f32[72,72]{1,0:T(8,128)S(1)}, f32[72,72]{1,0:T(8,128)}, u32[]{:S(2)}) copy-start(f32[72,72]{1,0:T(8,128)} %constant.16.clone.turn2) | copy-start | bytes 62212
  4.3 0.8 %copy-start.4 = (f32[72,128]{1,0:T(8,128)S(1)}, f32[72,128]{1,0:T(8,128)}, u32[]{:S(2)}) copy-start(f32[72,128]{1,0:T(8,128)} %constant.15.clone.sin2) | copy-start | bytes 110596
  5.0 0.8 %copy-start.5 = (f32[72,128]{1,0:T(8,128)S(1)}, f32[72,128]{1,0:T(8,128)}, u32[]{:S(2)}) copy-start(f32[72,128]{1,0:T(8,128)} %constant.14.clone.cos2) | copy-start | bytes 110596
  5.8 0.7 copy-start.6
  6.5 0.7 copy-start.7
  7.2 0.7 copy-start.8
  7.9 0.7 copy-start.9
  8.6 0.7 copy-start.10

commit v2 on v1

--- a/solution.py
+++ b/solution.py
@@ -50,8 +50,8 @@
     return tiles
 
 
-def kernel(n, spec, speed, wdir, turning, mask, along, across, cos2, sin2, turn2, lat,
-           out, refr, arrived, result, ex_in, ex_out, aligned, slots, cells, rolled, tabs, lat_tab, grid,
+def kernel(n, spec_hbm, speed_hbm, wdir_hbm, turning_hbm, mask_hbm, along_hbm, across_hbm, cos2_hbm, sin2_hbm,
+           turn2_hbm, lat_hbm, out, spec, speed, wdir, turning, mask, along, across, cos2, sin2, turn2, lat, loaded, refr, arrived, result, ex_in, ex_out, aligned, slots, cells, rolled, tabs, lat_tab, grid,
            mask_send, mask_recv, fwd_send, fwd_recv, back_send, back_recv,
            exf_send, exf_recv, exb_send, exb_recv):
     me = lax.axis_index("pts")
@@ -68,14 +68,32 @@
     extra = groups - n * (per_dev // 8)
     base = 8 * extra
 
-    def peer(i):
-        return lax.rem(me + i, n)
+    half = n // 2
+    operands = {
+        "mask": (mask_hbm, mask), "speed": (speed_hbm, speed), "wdir": (wdir_hbm, wdir),
+        "turning": (turning_hbm, turning), "spec": (spec_hbm, spec), "cos2": (cos2_hbm, cos2),
+        "sin2": (sin2_hbm, sin2), "turn2": (turn2_hbm, turn2), "lat": (lat_hbm, lat),
+        "along": (along_hbm, along), "across": (across_hbm, across),
+    }
+    loads = {name: pltpu.make_async_copy(src, dst, loaded.at[i]) for i, (name, (src, dst)) in enumerate(operands.items())}
+    for load in loads.values():
+        load.start()
+
+    def need(*names):
+        for name in names:
+            loads[name].wait()
 
     def each_peer(body):
-        def step(i, carry):
-            body(peer(i))
+        def far(i, carry):
+            body(half * (1 - me // half) + lax.rem(me + i, half))
             return carry
-        lax.fori_loop(1, n, step, 0)
+
+        def near(i, carry):
+            body(half * (me // half) + lax.rem(me + i, half))
+            return carry
+
+        lax.fori_loop(0, half, far, 0)
+        lax.fori_loop(1, half, near, 0)
 
     def remote(src, dst, send, recv, dev):
         return pltpu.make_async_remote_copy(src_ref=src, dst_ref=dst, send_sem=send, recv_sem=recv,
@@ -89,12 +107,15 @@
 
     barrier = pltpu.get_barrier_semaphore()
     each_peer(lambda p: pl.semaphore_signal(barrier, inc=1, device_id={"pts": p}, device_id_type=MESH))
+    need("mask")
     slots[me] = jnp.zeros((8, LANES), jnp.float32)
     slots[me, 0:band_rows, :] = mask[...].astype(jnp.float32)
 
+    need("speed", "wdir", "turning", "cos2", "sin2", "turn2")
     cos_w = speed[...] * jnp.cos(wdir[...])
     sin_w = speed[...] * jnp.sin(wdir[...])
     aligned[...] = cos2[:, 0:1] * cos_w + sin2[:, 0:1] * sin_w
+    need("spec")
     energy = jnp.sum(spec[...].reshape(comps // 8, 8, points), axis=0)
     energy = jnp.sum(energy, axis=0, keepdims=True) * (0.1 / comps)
     turn_col = turning[...]
@@ -117,10 +138,10 @@
     done = 0
 
     def source_to(row_end, done):
-        need = -(-row_end // PAIR)
-        if need > done:
-            lax.fori_loop(done, need, source, 0)
-        return max(need, done)
+        end = -(-row_end // PAIR)
+        if end > done:
+            lax.fori_loop(done, end, source, 0)
+        return max(end, done)
 
     done = source_to(base, done)
     for p in range(extra):
@@ -138,6 +159,7 @@
                                    fwd_send.at[c], fwd_recv.at[c], p).start())
         arrived[c, me] = refr[rows_of(first + CHUNK * me, CHUNK), :]
 
+    need("lat", "along", "across")
     others = pl.ds(0, n - 1)
     wait_bytes(slots.at[others], mask_recv)
     for b in range(n):
@@ -284,12 +306,16 @@
     vmem = pl.BlockSpec(memory_space=pltpu.VMEM)
     dma = pltpu.SemaphoreType.DMA
     f32, i32 = jnp.float32, jnp.int32
+    line = lambda v: v.reshape(1, points)
+    operands = (spectrum, line(wind_speed), line(wind_dir), line(turning), sea_mask, *spectral_tables(), lat)
     call = pl.pallas_call(
         functools.partial(kernel, n),
         out_shape=jax.ShapeDtypeStruct((comps, points), f32),
-        in_specs=[vmem] * 11,
+        in_specs=[pl.BlockSpec(memory_space=pltpu.HBM)] * 11,
         out_specs=vmem,
         scratch_shapes=[
+            *(pltpu.VMEM(x.shape, x.dtype) for x in operands),
+            dma((11,)),
             pltpu.VMEM((comps, points), f32),
             pltpu.VMEM((chunks, n, CHUNK, points), f32),
             pltpu.VMEM((chunks, n, CHUNK, points), f32),
@@ -307,11 +333,10 @@
             dma((extra,)), dma, dma, dma((extra,)),
         ],
         compiler_params=pltpu.CompilerParams(
-            collective_id=0, has_side_effects=True, vmem_limit_bytes=40 * 1024 * 1024
+            collective_id=0, has_side_effects=True, vmem_limit_bytes=60 * 1024 * 1024
         ),
     )
-    line = lambda v: v.reshape(1, points)
-    return call(spectrum, line(wind_speed), line(wind_dir), line(turning), sea_mask, *spectral_tables(), lat)
+    return call(*operands)
 
 
 def solution(mesh):

time: 75.4 us -> 70 us (0.928); the launches traced: 74.2 us -> 69.8 us
  local copies, waits for them, and re-layouts: 10.3 us -> 2.47 us
  Pallas kernels: 63.9 us -> 67.3 us
    unnamed x23 -> x1, local copies, waits for them, and re-layouts: 10.3 us -> 2.47 us
    pallas_call x1, Pallas kernels: 63.9 us -> 67.3 us  [shards(): return call(*operands)]
where the time goes in v2:
time: 70 us; the launch traced here: 69.8 us
  Pallas kernels  67.3 us (96%)
  local copies, waits for them, and re-layouts  2.47 us (4%)
    pallas_call x1, Pallas kernels, shards(): return call(*operands)  67.3 us
    unnamed x1, local copies, waits for them, and re-layouts  2.47 us

profile of v2, /device:TPU:0, one launch (start us, length us, event | category | flops | bytes accessed | tf_op | source)
XLA Modules:
  0.0 69.8 jit_solution(6836232484552023851)
XLA Ops:
  0.0 67.3 %shard_map.109 = f32[1296,256]{1,0:T(8,128)} custom-call(f32[1296,256]{1,0:T(8,128)} %spec_hbm.1, f32[1,256]{1,0:T(1,128)} %bitcast.3, f32[1,256]{1,0:T(1,128)} %bitcast.4, f32[1,256]{1,0:T(1,128)} %bitcast.5, s32[3,128]{1,0:T(4,128)} %mask_hbm.1, f32[1296,128]{1,0:T(8,128)} %constant.12.clone.along_hbm, f32[1296,128]{1,0:T(8,128)} %constant.13.clone.across_hbm, ...), custom_call_target="tpu_custom_call" | custom-call | tf_op jit(solution)/shard_map/pallas_call | solution.py:339
  67.4 2.5 %copy.13 = f32[1296,256]{1,0:T(8,128)} copy(f32[1296,256]{1,0:T(8,128)} %shard_map.109) | data formatting | bytes 2654208

commit v3 on v2

--- a/solution.py
+++ b/solution.py
@@ -53,7 +53,7 @@
 def kernel(n, spec_hbm, speed_hbm, wdir_hbm, turning_hbm, mask_hbm, along_hbm, across_hbm, cos2_hbm, sin2_hbm,
            turn2_hbm, lat_hbm, out, spec, speed, wdir, turning, mask, along, across, cos2, sin2, turn2, lat, loaded, refr, arrived, result, ex_in, ex_out, aligned, slots, cells, rolled, tabs, lat_tab, grid,
            mask_send, mask_recv, fwd_send, fwd_recv, back_send, back_recv,
-           exf_send, exf_recv, exb_send, exb_recv):
+           exf_send, exf_recv, exb_send, exb_recv, own):
     me = lax.axis_index("pts")
     comps, points = spec.shape
     band_rows = mask.shape[0]
@@ -262,7 +262,7 @@
             wait_bytes(ex_in.at[others], exf_recv)
             advance(ex_in, ex_out, 0, 8 * me)
             each_peer(lambda p: remote(ex_out.at[p], out.at[rows_of(8 * me, 8)], exb_send, exb_recv.at[me], p).start())
-            out[rows_of(8 * me, 8), :] = ex_out[me]
+            pltpu.make_async_copy(ex_out.at[me], out.at[rows_of(8 * me, 8)], own.at[chunks]).start()
 
     def one_chunk(c, carry):
         wait_bytes(arrived.at[c, others], fwd_recv.at[c])
@@ -271,7 +271,7 @@
             advance(arrived.at[c], result.at[c], sub, mine + 8 * sub)
         each_peer(lambda p: remote(result.at[c, p], out.at[rows_of(mine, CHUNK)],
                                    back_send.at[c], back_recv.at[c], p).start())
-        out[rows_of(mine, CHUNK), :] = result[c, me]
+        pltpu.make_async_copy(result.at[c, me], out.at[rows_of(mine, CHUNK)], own.at[c]).start()
         return carry
 
     lax.fori_loop(0, chunks, one_chunk, 0)
@@ -281,6 +281,7 @@
         wait_bytes(arrived.at[c, others], fwd_send.at[c])
         wait_bytes(result.at[c, others], back_send.at[c])
         wait_bytes(result.at[c, others], back_recv.at[c])
+        wait_bytes(result.at[c, 0], own.at[c])
     if extra:
         for p in range(extra):
             @pl.when(me != p)
@@ -291,6 +292,7 @@
         @pl.when(me < extra)
         def _():
             wait_bytes(ex_out.at[others], exb_send)
+            wait_bytes(ex_out.at[0], own.at[chunks])
 
 
 def shards(n, spectrum, wind_speed, wind_dir, turning, sea_mask, band_start):
@@ -303,7 +305,6 @@
     extra = max(groups - n * (groups // n), 1)
     latitude = (-60.0 + 120.0 * (np.arange(rows) + 0.5) / rows) * (math.pi / 180.0)
     lat = np.ascontiguousarray(np.broadcast_to((1.0 / np.cos(latitude))[:, None], (rows, LANES))).astype(np.float32)
-    vmem = pl.BlockSpec(memory_space=pltpu.VMEM)
     dma = pltpu.SemaphoreType.DMA
     f32, i32 = jnp.float32, jnp.int32
     line = lambda v: v.reshape(1, points)
@@ -312,7 +313,7 @@
         functools.partial(kernel, n),
         out_shape=jax.ShapeDtypeStruct((comps, points), f32),
         in_specs=[pl.BlockSpec(memory_space=pltpu.HBM)] * 11,
-        out_specs=vmem,
+        out_specs=pl.BlockSpec(memory_space=pl.ANY),
         scratch_shapes=[
             *(pltpu.VMEM(x.shape, x.dtype) for x in operands),
             dma((11,)),
@@ -330,7 +331,7 @@
             pltpu.VMEM((CHUNK // 8, tiles, 8, LANES), f32),
             dma, dma,
             dma((chunks,)), dma((chunks,)), dma((chunks,)), dma((chunks,)),
-            dma((extra,)), dma, dma, dma((extra,)),
+            dma((extra,)), dma, dma, dma((extra,)), dma((chunks + 1,)),
         ],
         compiler_params=pltpu.CompilerParams(
             collective_id=0, has_side_effects=True, vmem_limit_bytes=60 * 1024 * 1024

time: 70 us -> 69.1 us (0.987)
  Pallas kernels: 67.3 us -> 66.4 us
    pallas_call x1, Pallas kernels: 67.3 us -> 66.4 us  [shards(): return call(*operands)]
where the time goes in v3:
time: 69.1 us; the launch traced here: 68.9 us
  Pallas kernels  66.4 us (96%)
  local copies, waits for them, and re-layouts  2.47 us (4%)
    pallas_call x1, Pallas kernels, shards(): return call(*operands)  66.4 us
    unnamed x1, local copies, waits for them, and re-layouts  2.47 us

profile of v3, /device:TPU:0, one launch (start us, length us, event | category | flops | bytes accessed | tf_op | source)
XLA Modules:
  0.0 68.9 jit_solution(1820386332632785559)
XLA Ops:
  0.0 66.4 %shard_map.109 = f32[1296,256]{1,0:T(8,128)} custom-call(f32[1296,256]{1,0:T(8,128)} %spec_hbm.1, f32[1,256]{1,0:T(1,128)} %bitcast.3, f32[1,256]{1,0:T(1,128)} %bitcast.4, f32[1,256]{1,0:T(1,128)} %bitcast.5, s32[3,128]{1,0:T(4,128)} %mask_hbm.1, f32[1296,128]{1,0:T(8,128)} %constant.12.clone.along_hbm, f32[1296,128]{1,0:T(8,128)} %constant.13.clone.across_hbm, ...), custom_call_target="tpu_custom_call" | custom-call | tf_op jit(solution)/shard_map/pallas_call | solution.py:340
  66.4 2.5 %copy.13 = f32[1296,256]{1,0:T(8,128)} copy(f32[1296,256]{1,0:T(8,128)} %shard_map.109) | data formatting | bytes 2654208

commit v4 on v3

--- a/solution.py
+++ b/solution.py
@@ -311,7 +311,7 @@
     operands = (spectrum, line(wind_speed), line(wind_dir), line(turning), sea_mask, *spectral_tables(), lat)
     call = pl.pallas_call(
         functools.partial(kernel, n),
-        out_shape=jax.ShapeDtypeStruct((comps, points), f32),
+        out_shape=pltpu.VMEM((comps, points), f32),
         in_specs=[pl.BlockSpec(memory_space=pltpu.HBM)] * 11,
         out_specs=pl.BlockSpec(memory_space=pl.ANY),
         scratch_shapes=[
@@ -334,7 +334,7 @@
             dma((extra,)), dma, dma, dma((extra,)), dma((chunks + 1,)),
         ],
         compiler_params=pltpu.CompilerParams(
-            collective_id=0, has_side_effects=True, vmem_limit_bytes=60 * 1024 * 1024
+            collective_id=0, has_side_effects=True, vmem_limit_bytes=58 * 1024 * 1024
         ),
     )
     return call(*operands)

time: 69.1 us -> 67.6 us (0.978)
  local copies, waits for them, and re-layouts: 2.47 us -> 1.06 us
    unnamed x1, local copies, waits for them, and re-layouts: 2.47 us -> 1.06 us
where the time goes in v4:
time: 67.6 us; the launch traced here: 67.4 us
  Pallas kernels  66.3 us (98%)
  local copies, waits for them, and re-layouts  1.06 us (2%)
    pallas_call x1, Pallas kernels, shards(): return call(*operands)  66.3 us

profile of v4, /device:TPU:0, one launch (start us, length us, event | category | flops | bytes accessed | tf_op | source)
XLA Modules:
  0.0 67.4 jit_solution(2814090357414808314)
XLA Ops:
  0.0 66.3 %shard_map.109 = f32[1296,256]{1,0:T(8,128)S(1)} custom-call(f32[1296,256]{1,0:T(8,128)} %spec_hbm.1, f32[1,256]{1,0:T(1,128)} %bitcast.3, f32[1,256]{1,0:T(1,128)} %bitcast.4, f32[1,256]{1,0:T(1,128)} %bitcast.5, s32[3,128]{1,0:T(4,128)} %mask_hbm.1, f32[1296,128]{1,0:T(8,128)} %constant.12.clone.along_hbm, f32[1296,128]{1,0:T(8,128)} %constant.13.clone.across_hbm, ...), custom_call_target="tpu_custom_call" | custom-call | tf_op jit(solution)/shard_map/pallas_call | solution.py:340
  66.3 1.1 %copy.13 = f32[1296,256]{1,0:T(8,128)} copy(f32[1296,256]{1,0:T(8,128)S(1)} %shard_map.109) | data formatting | bytes 2654208
